TPU v7x, 32 devices: a whole 2x2x4 slice. The times are simulated.
32 devices in a mesh: dp: 4 (over y, x), ctx: 8 (over z, core).
Axes of the slice: x: 2, y: 2, z: 4, core: 2. Of those that a mesh axis runs over, the one named last changes fastest.
Arguments:
- queries: bfloat16 [4096, 1024], P(('dp', 'ctx')), parts along dimension 0, may hold values from -8 to 8
- keys: bfloat16 [4096, 1024], P(('dp', 'ctx')), parts along dimension 0, may hold values from -6 to 6
- values: bfloat16 [4096, 1024], P(('dp', 'ctx')), parts along dimension 0, may hold values from -6 to 6
- cotangent: bfloat16 [4096, 1024], P(('dp', 'ctx')), parts along dimension 0, may hold values from -0.796875 to 0.796875
- out_weight: bfloat16 [1024, 1024], P('ctx'), may hold values from -0.75 to 0.75
Outputs:
- projected: bfloat16 [4096, 1024], P(('dp', 'ctx')), parts along dimension 0
- weight_grad: float32 [4096, 1024], P(('dp', 'ctx')), parts along dimension 0
- query_grad: bfloat16 [4096, 1024], P(('dp', 'ctx')), parts along dimension 0
- key_grad: bfloat16 [4096, 1024], P(('dp', 'ctx')), parts along dimension 0
- value_grad: bfloat16 [4096, 1024], P(('dp', 'ctx')), parts along dimension 0
There are 4 independent parts, one for each index of `dp`. A program takes and returns all parts, laid end to end along the dimension named above; an argument that names none is the same for every part. Nothing has to cross between parts.
All inputs are finite; a program needn't handle non-finite values.
Results may differ from a plain program's by a relative error of at most 0.034.
Values may be sent and summed in bfloat16 or wider, within the bound.
A program may use at most 64 MiB of HBM per device.

v0:
```python
import jax
import jax.numpy as jnp
from jax import lax
from jax.sharding import PartitionSpec as P

H = 16
DH = 64
R = 16


def partner_2(value, axis, apart):
    mask = 2**apart
    pairs = [(source, source ^ mask) for source in range(lax.axis_size(axis))]
    return lax.ppermute(value, axis, pairs)


def select_mask(dtype):
    residue = jnp.arange(R)[:, None]
    head_ids = jnp.arange(H)[None, :]
    return (head_ids % R == residue).astype(dtype)[:, :, None]


def sparse_rows(full_rows):
    reshaped = full_rows.reshape(full_rows.shape[0] // R, R, H, DH)
    return jnp.sum(reshaped * select_mask(full_rows.dtype), axis=1)


def dense_rows(sparse):
    placed = sparse[:, None, :, :] * select_mask(sparse.dtype)
    return placed.reshape(sparse.shape[0] * R, H * DH)


def spread(payload, swapper, bit_list, device_index):
    visited = []
    gathered = payload
    for bit_num in bit_list:
        partner = swapper(gathered, bit_num)
        upper_half = device_index // (1 << bit_num) % 2 == 1
        gathered = jnp.where(
            upper_half, jnp.stack([partner, gathered]), jnp.stack([gathered, partner])
        )
        visited.insert(0, bit_num)
    axis_order = [visited.index(bit_num) for bit_num in sorted(visited, reverse=True)]
    trailing = list(range(len(visited), gathered.ndim))
    gathered = jnp.transpose(gathered, axis_order + trailing)
    return gathered.reshape((-1,) + payload.shape[1:])


def shards(queries, keys, values, cotangent, out_weight):
    ctx_size = lax.axis_size("ctx")
    seg_devices = min(64, ctx_size // 2)
    seg_bits = seg_devices.bit_length() - 1
    device_index = lax.axis_index("ctx")
    bit_list = list(range(seg_bits))
    score_scale = DH ** (-0.5)
    q_sparse = sparse_rows(queries)
    k_sparse = sparse_rows(keys)
    v_sparse = sparse_rows(values)
    gathered = spread(
        jnp.stack([k_sparse, v_sparse], axis=1),
        lambda payload, bit_num: partner_2(payload, "ctx", bit_num),
        bit_list,
        device_index,
    )
    seg_keys = gathered[:, 0]
    seg_values = gathered[:, 1]
    full_weight = lax.all_gather(out_weight, "ctx", axis=0, tiled=True)
    scores = (
        jnp.einsum("qhd,khd->hqk", q_sparse, seg_keys, preferred_element_type=jnp.float32)
        * score_scale
    )
    row_top = jnp.max(scores, axis=-1, keepdims=True)
    log_total = row_top + jnp.log(jnp.sum(jnp.exp(scores - row_top), axis=-1, keepdims=True))
    probability = jnp.exp(scores - log_total)
    attn_sparse = jnp.einsum(
        "hqk,khd->qhd",
        probability.astype(jnp.bfloat16),
        seg_values,
        preferred_element_type=jnp.float32,
    ).astype(jnp.bfloat16)
    attention = dense_rows(attn_sparse)
    projected = lax.dot_general(
        attention, full_weight, (((1,), (1,)), ((), ())), preferred_element_type=jnp.float32
    ).astype(jnp.bfloat16)
    weight_grad = lax.psum_scatter(
        lax.dot_general(
            cotangent, attention, (((0,), (0,)), ((), ())), preferred_element_type=jnp.float32
        ),
        "ctx",
        scatter_dimension=0,
        tiled=True,
    )
    d_attention = jnp.dot(cotangent, full_weight, preferred_element_type=jnp.float32).astype(
        jnp.bfloat16
    )
    da_sparse = sparse_rows(d_attention)
    row_delta = jnp.sum(da_sparse.astype(jnp.float32) * attn_sparse.astype(jnp.float32), axis=-1)
    prob_grad = jnp.einsum(
        "qhd,khd->hqk", da_sparse, seg_values, preferred_element_type=jnp.float32
    )
    score_grad = (probability * (prob_grad - row_delta.T[:, :, None])).astype(jnp.bfloat16)
    query_part = (
        jnp.einsum("hqk,khd->qhd", score_grad, seg_keys, preferred_element_type=jnp.float32)
        * score_scale
    ).astype(jnp.bfloat16)
    row_stats = jnp.stack([log_total[:, :, 0].T, row_delta], axis=1)
    seg_stats = spread(
        row_stats,
        lambda payload, bit_num: partner_2(payload, "ctx", bit_num),
        bit_list,
        device_index,
    )
    paired = spread(
        jnp.stack([q_sparse, da_sparse], axis=1),
        lambda payload, bit_num: partner_2(payload, "ctx", bit_num),
        bit_list,
        device_index,
    )
    seg_queries = paired[:, 0]
    seg_cotangent = paired[:, 1]
    key_scores = (
        jnp.einsum("qhd,khd->hqk", seg_queries, k_sparse, preferred_element_type=jnp.float32)
        * score_scale
    )
    key_prob = jnp.exp(key_scores - seg_stats[:, 0].T[:, :, None])
    key_dgrad = jnp.einsum(
        "qhd,khd->hqk", seg_cotangent, v_sparse, preferred_element_type=jnp.float32
    )
    key_dscore = (key_prob * (key_dgrad - seg_stats[:, 1].T[:, :, None])).astype(jnp.bfloat16)
    key_part = (
        jnp.einsum("hqk,qhd->khd", key_dscore, seg_queries, preferred_element_type=jnp.float32)
        * score_scale
    ).astype(jnp.bfloat16)
    value_part = jnp.einsum(
        "hqk,qhd->khd",
        key_prob.astype(jnp.bfloat16),
        seg_cotangent,
        preferred_element_type=jnp.float32,
    ).astype(jnp.bfloat16)
    return (
        projected,
        weight_grad,
        dense_rows(query_part),
        dense_rows(key_part),
        dense_rows(value_part),
    )


def solution(mesh):
    in_specs = (
        P(("dp", "ctx"), None),
        P(("dp", "ctx"), None),
        P(("dp", "ctx"), None),
        P(("dp", "ctx"), None),
        P("ctx", None),
    )
    out_specs = (
        P(("dp", "ctx"), None),
        P(("dp", "ctx"), None),
        P(("dp", "ctx"), None),
        P(("dp", "ctx"), None),
        P(("dp", "ctx"), None),
    )
    return jax.shard_map(shards, mesh=mesh, in_specs=in_specs, out_specs=out_specs, check_vma=False)
```

profile of v0, /device:TPU:0, one launch (start us, length us, event | category | flops | bytes accessed | tf_op | source)
XLA Modules:
  0.0 124.3 jit_solution(6915488580610237920)
XLA Ops:
  7.2 0.0 copy-start
  7.2 0.0 all-gather.2.cloned.1.call-start
  7.2 0.7 all-gather.2.cloned.1.call-update
  7.9 0.0 reduce-scatter.2.cloned.1.call-start
  8.0 1.3 %reshape.286 = bf16[8,16,16,64]{3,2,1,0:T(8,128)(2,1)S(1)} reshape(bf16[128,1024]{1,0:T(8,128)(2,1)} %param.5) | data formatting | bytes 524288 | tf_op jit(solution)/shard_map/reshape | solution.py:24
  9.3 1.3 %reshape.284 = bf16[8,16,16,64]{3,2,1,0:T(8,128)(2,1)S(1)} reshape(bf16[128,1024]{1,0:T(8,128)(2,1)} %param.6) | data formatting | bytes 524288 | tf_op jit(solution)/shard_map/reshape | solution.py:24
  10.7 1.3 %reshape.285 = bf16[8,16,16,64]{3,2,1,0:T(8,128)(2,1)S(1)} reshape(bf16[128,1024]{1,0:T(8,128)(2,1)} %param.7) | data formatting | bytes 524288 | tf_op jit(solution)/shard_map/reshape | solution.py:24
  12.0 29.4 %all-gather.2.cloned.1.call-done = bf16[1024,1024]{1,0:T(8,128)(2,1)} async-done(((bf16[128,1024]{1,0:T(8,128)(2,1)}), bf16[1024,1024]{1,0:T(8,128)(2,1)}) %all-gather.2.cloned.1.call-update) | async-done | bytes 2097168 | tf_op jit(solution)/shard_map/all_gather | solution.py:67
  41.4 0.0 copy-done
  41.5 2.0 %convolution_convert_fusion = bf16[128,1024]{1,0:T(8,128)(2,1)S(1)} fusion(bf16[128,1024]{1,0:T(8,128)(2,1)S(1)} %copy-done, bf16[1024,1024]{1,0:T(8,128)(2,1)} %all-gather.2.cloned.1.call-done), kind=kOutput, calls=%fused_computation.1 | convolution fusion | flops 268566528 | bytes 2621440 | tf_op jit(solution)/shard_map/dot_general | solution.py:93
  43.5 0.3 reshape.287
  43.8 0.6 multiply_reduce_fusion
  44.5 0.3 collective-permute-start.2
  44.8 0.3 collective-permute-start
  45.1 0.7 collective-permute-done.2
  45.9 1.5 %collective-permute-start.3 = (bf16[2,8,2,16,64]{4,3,1,2,0:T(8,128)(2,1)S(1)}, bf16[2,8,2,16,64]{4,3,1,2,0:T(8,128)(2,1)S(1)}, u32[]{:S(2)}, u32[]{:S(2)}) collective-permute-start(bf16[2,8,2,16,64]{4,3,1,2,0:T(8,128)(2,1)S(1)} %maximum_select_fusion.4), channel_id=1, source_target_pairs={{0,2},{1,3},{2,0},{3,1},{4,6},{5,7},{6,4},{7,5},{8,10},{9,11},{10,... | collective-permute-start | bytes 196616 | tf_op jit(solution)/shard_map/ppermute | solution.py:14
  47.4 0.0 collective-permute-done
  47.4 0.6 collective-permute-start.1
  48.2 4.1 %collective-permute-done.3 = bf16[2,8,2,16,64]{4,3,1,2,0:T(8,128)(2,1)S(1)} collective-permute-done((bf16[2,8,2,16,64]{4,3,1,2,0:T(8,128)(2,1)S(1)}, bf16[2,8,2,16,64]{4,3,1,2,0:T(8,128)(2,1)S(1)}, u32[]{:S(2)}, u32[]{:S(2)}) %collective-permute-start.3) | collective-permute-done | bytes 65568 | tf_op jit(solution)/shard_map/ppermute | solution.py:14
  52.3 0.1 maximum_select_fusion.1
  52.4 2.0 %collective-permute-done.1 = bf16[2,8,2,16,64]{4,3,1,2,0:T(8,128)(2,1)S(1)} collective-permute-done((bf16[2,8,2,16,64]{4,3,1,2,0:T(8,128)(2,1)S(1)}, bf16[2,8,2,16,64]{4,3,1,2,0:T(8,128)(2,1)S(1)}, u32[]{:S(2)}, u32[]{:S(2)}) %collective-permute-start.1) | collective-permute-done | bytes 65568 | tf_op jit(solution)/shard_map/ppermute | solution.py:14
  54.4 0.1 maximum_select_fusion
  54.5 0.1 copy.34
  54.5 0.2 fusion.33
  54.8 0.2 exponential_reduce_fusion
  55.0 0.3 multiply_reduce_fusion.4
  55.3 0.1 copy.43
  55.4 0.1 copy.44
  55.4 0.3 fusion.11
  55.7 0.1 collective-permute-start.4
  55.9 1.1 collective-permute-done.4
  57.0 1.5 %collective-permute-start.5 = (f32[2,8,2,16]{3,1,2,0:T(8,128)S(1)}, f32[2,8,2,16]{3,1,2,0:T(8,128)S(1)}, u32[]{:S(2)}, u32[]{:S(2)}) collective-permute-start(f32[2,8,2,16]{3,1,2,0:T(8,128)S(1)} %maximum_select_fusion.7), channel_id=1, source_target_pairs={{0,2},{1,3},{2,0},{3,1},{4,6},{5,7},{6,4},{7,5},{8,10},{9,11},{10,... | collective-permute-start | bytes 6152 | tf_op jit(solution)/shard_map/ppermute | solution.py:14
  58.5 2.2 %collective-permute-done.5 = f32[2,8,2,16]{3,1,2,0:T(8,128)S(1)} collective-permute-done((f32[2,8,2,16]{3,1,2,0:T(8,128)S(1)}, f32[2,8,2,16]{3,1,2,0:T(8,128)S(1)}, u32[]{:S(2)}, u32[]{:S(2)}) %collective-permute-start.5) | collective-permute-done | bytes 2080 | tf_op jit(solution)/shard_map/ppermute | solution.py:14
  60.7 0.1 copy.49
  60.8 0.1 copy.46
  60.9 0.2 fusion.2
  61.1 0.2 fusion.9
  61.2 0.3 fusion.10
  61.6 1.2 broadcast_multiply_fusion
  62.8 0.3 mul.137
  63.1 2.7 %convolution_bitcast_fusion = f32[1024,1024]{0,1:T(8,128)} fusion(bf16[128,1024]{1,0:T(8,128)(2,1)S(1)} %mul.137, bf16[128,1024]{1,0:T(8,128)(2,1)S(1)} %copy-done), kind=kOutput, calls=%fused_computation | convolution fusion | flops 268435456 | bytes 4718592 | tf_op jit(solution)/shard_map/dot_general | solution.py:86
  65.8 0.0 reduce-scatter.2.cloned.1.call-update
  65.8 2.3 %mul.154 = bf16[128,1024]{1,0:T(8,128)(2,1)} reshape(bf16[8,16,16,64]{3,2,1,0:T(8,128)(2,1)} %get-tuple-element.37) | data formatting | bytes 524288 | tf_op jit(solution)/shard_map/mul | solution.py:29
  68.1 2.1 %mul.144 = bf16[128,1024]{1,0:T(8,128)(2,1)} reshape(bf16[8,16,16,64]{3,2,1,0:T(8,128)(2,1)} %get-tuple-element.38) | data formatting | bytes 524288 | tf_op jit(solution)/shard_map/mul | solution.py:29
  70.3 1.1 mul.151
  71.3 1.5 %convolution_convert_fusion.1 = bf16[128,1024]{1,0:T(8,128)(2,1)} fusion(bf16[128,1024]{1,0:T(8,128)(2,1)S(1)} %mul.137, bf16[1024,1024]{1,0:T(8,128)(2,1)S(1)} %copy-done.1), kind=kOutput, calls=%fused_computation.2 | convolution fusion | flops 268566528 | bytes 2621440 | tf_op jit(solution)/shard_map/dot_general | solution.py:82
  72.8 42.6 %reduce-scatter.2.cloned.1.call-done = f32[128,1024]{0,1:T(8,128)} async-done(((f32[1024,1024]{0,1:T(8,128)}), f32[128,1024]{0,1:T(8,128)}) %reduce-scatter.2.cloned.1.call-update) | async-done | bytes 524304 | tf_op jit(solution)/shard_map/reduce_scatter | solution.py:85
  115.5 2.0 %copy.52 = f32[128,1024]{1,0:T(8,128)} copy(f32[128,1024]{0,1:T(8,128)} %reduce-scatter.2.cloned.1.call-done) | data formatting | bytes 1048576
  (23 shorter events, 0.4 us)
Async XLA Ops:
  7.2 34.3 %copy-start = (bf16[128,1024]{1,0:T(8,128)(2,1)S(1)}, bf16[128,1024]{1,0:T(8,128)(2,1)}, u32[]{:S(2)}) copy-start(bf16[128,1024]{1,0:T(8,128)(2,1)} %param.8) | copy-start | bytes 786436
  7.2 34.3 %all-gather.2.cloned.1.call-start = ((), (), s32[]{:S(2)}) async-start(), calls=%async_computation.1 | async-start | bytes 2359296 | tf_op jit(solution)/shard_map/all_gather | solution.py:67
  7.9 107.6 %reduce-scatter.2.cloned.1.call-start = ((), (), s32[]{:S(2)}) async-start(), calls=%async_computation.2 | async-start | bytes 4718592 | tf_op jit(solution)/shard_map/reduce_scatter | solution.py:85
  44.5 1.3 %collective-permute-start.2 = (bf16[8,2,16,64]{3,2,0,1:T(8,128)(2,1)S(1)}, bf16[8,2,16,64]{3,2,0,1:T(8,128)(2,1)S(1)}, u32[]{:S(2)}, u32[]{:S(2)}) collective-permute-start(bf16[8,2,16,64]{3,2,0,1:T(8,128)(2,1)S(1)} %get-tuple-element.28), channel_id=1, source_target_pairs={{0,1},{1,0},{2,3},{3,2},{4,5},{5,4},{6,7},{7,6},{8,9},{9,8},{10,11... | collective-permute-start | bytes 98312 | tf_op jit(solution)/shard_map/ppermute | solution.py:14
  44.8 2.6 %collective-permute-start = (bf16[8,2,16,64]{3,2,0,1:T(8,128)(2,1)S(1)}, bf16[8,2,16,64]{3,2,0,1:T(8,128)(2,1)S(1)}, u32[]{:S(2)}, u32[]{:S(2)}) collective-permute-start(bf16[8,2,16,64]{3,2,0,1:T(8,128)(2,1)S(1)} %get-tuple-element.31), channel_id=1, source_target_pairs={{0,1},{1,0},{2,3},{3,2},{4,5},{5,4},{6,7},{7,6},{8,9},{9,8},{10,11... | collective-permute-start | bytes 98312 | tf_op jit(solution)/shard_map/ppermute | solution.py:14
  45.9 6.4 %collective-permute-start.3 = (bf16[2,8,2,16,64]{4,3,1,2,0:T(8,128)(2,1)S(1)}, bf16[2,8,2,16,64]{4,3,1,2,0:T(8,128)(2,1)S(1)}, u32[]{:S(2)}, u32[]{:S(2)}) collective-permute-start(bf16[2,8,2,16,64]{4,3,1,2,0:T(8,128)(2,1)S(1)} %maximum_select_fusion.4), channel_id=1, source_target_pairs={{0,2},{1,3},{2,0},{3,1},{4,6},{5,7},{6,4},{7,5},{8,10},{9,11},{10,... | collective-permute-start | bytes 196616 | tf_op jit(solution)/shard_map/ppermute | solution.py:14
  47.4 6.9 %collective-permute-start.1 = (bf16[2,8,2,16,64]{4,3,1,2,0:T(8,128)(2,1)S(1)}, bf16[2,8,2,16,64]{4,3,1,2,0:T(8,128)(2,1)S(1)}, u32[]{:S(2)}, u32[]{:S(2)}) collective-permute-start(bf16[2,8,2,16,64]{4,3,1,2,0:T(8,128)(2,1)S(1)} %maximum_select_fusion.2), channel_id=1, source_target_pairs={{0,2},{1,3},{2,0},{3,1},{4,6},{5,7},{6,4},{7,5},{8,10},{9,11},{10,... | collective-permute-start | bytes 196616 | tf_op jit(solution)/shard_map/ppermute | solution.py:14
  55.7 1.2 collective-permute-start.4
  57.0 3.7 %collective-permute-start.5 = (f32[2,8,2,16]{3,1,2,0:T(8,128)S(1)}, f32[2,8,2,16]{3,1,2,0:T(8,128)S(1)}, u32[]{:S(2)}, u32[]{:S(2)}) collective-permute-start(f32[2,8,2,16]{3,1,2,0:T(8,128)S(1)} %maximum_select_fusion.7), channel_id=1, source_target_pairs={{0,2},{1,3},{2,0},{3,1},{4,6},{5,7},{6,4},{7,5},{8,10},{9,11},{10,... | collective-permute-start | bytes 6152 | tf_op jit(solution)/shard_map/ppermute | solution.py:14
  65.8 5.5 %copy-start.1 = (bf16[1024,1024]{1,0:T(8,128)(2,1)S(1)}, bf16[1024,1024]{1,0:T(8,128)(2,1)}, u32[]{:S(2)}) copy-start(bf16[1024,1024]{1,0:T(8,128)(2,1)} %all-gather.2.cloned.1.call-done) | copy-start | bytes 6291460
Sparse Core Ops, SparseCore 0:
  9.6 31.7 all-gather.1
  65.9 49.4 reduce-scatter.1
where the time goes:
time: 125 us; the launch traced here: 124 us
  waiting for transfers between devices  82.8 us (66%)
  between operations  14.3 us (11%)
  local copies, waits for them, and re-layouts  12.6 us (10%)
  matrix products  7.71 us (6%)
  starting transfers between devices  4.43 us (4%)
  other arithmetic  2.47 us (2%)
    reduce_scatter x1, waiting for transfers between devices, shards(): lax.psum_scatter(lax.dot_general(cotangent, attention, (((0,), (0,)), (()...  42.6 us
    all_gather x1, waiting for transfers between devices, shards(): full_weight = lax.all_gather(out_weight, 'ctx', axis=0, tiled=True)  29.4 us
    ppermute x6, waiting for transfers between devices, partner_2(): return lax.ppermute(value, axis, pairs)  10.1 us
    mul x4, local copies, waits for them, and re-layouts, dense_rows(): placed = sparse[:, None, :, :] * select_mask(sparse.dtype)  5.82 us
    ppermute x6, starting transfers between devices, partner_2(): return lax.ppermute(value, axis, pairs)  4.36 us
    reshape x4, local copies, waits for them, and re-layouts, sparse_rows(): reshaped = full_rows.reshape(full_rows.shape[0] // R, R, H, DH)  4.33 us
    dot_general x1, matrix products, shards(): lax.dot_general(cotangent, attention, (((0,), (0,)), ((), ())), preferred...  2.66 us
  transfers between devices with their start and end apart: 8, of which 7 were waited for; matrix products, arithmetic and copies ran while one was open for 9% of the time, Pallas kernels for 0%

commit v1 on v0

--- a/solution.py
+++ b/solution.py
@@ -1,6 +1,10 @@
+import functools
+
 import jax
 import jax.numpy as jnp
 from jax import lax
+from jax.experimental import pallas as pl
+from jax.experimental.pallas import tpu as pltpu
 from jax.sharding import PartitionSpec as P
 
 H = 16
@@ -146,6 +150,277 @@
     )
 
 
+LANES = 128
+D = H * DH
+F32 = jnp.float32
+BF16 = jnp.bfloat16
+
+
+def fits(mesh):
+    return mesh.shape["ctx"] * LANES == D
+
+
+def mm(a, b, dims):
+    return lax.dot_general(a, b, (dims, ((), ())), preferred_element_type=F32)
+
+
+NN = ((1,), (0,))
+NT = ((1,), (1,))
+TN = ((0,), (0,))
+
+
+def fused_kernel(
+    n, rows,
+    q_hbm, k_hbm, v_hbm, c_hbm, w_hbm,
+    proj_hbm, wg_hbm, dq_hbm, dk_hbm, dv_hbm,
+    q_v, k_v, v_v, c_v, w_v,
+    qkv_send, qkv_recv, cot_send, cot_recv, attn_recv, da_send, da_recv,
+    pr_send, pr_recv, dg_send, dg_recv, attn2,
+    pr_out, wg_out, dq_out, dk_out, dv_out,
+    send_sem, recv_sem, in_sem, out_sem,
+):
+    per = rows // R
+    group = 2 * per
+    seg_devices = n // 2
+    total = n * per
+    me = lax.axis_index("ctx")
+    peers = [lax.rem(me + d, n) for d in range(n)]
+    sources = [lax.rem(me + n - d, n) for d in range(n)]
+
+    barrier = pltpu.get_barrier_semaphore()
+    for d in range(1, n):
+        pl.semaphore_signal(
+            barrier, inc=1, device_id={"ctx": peers[d]}, device_id_type=pl.DeviceIdType.MESH
+        )
+    loads = [
+        pltpu.make_async_copy(src, dst, in_sem.at[i])
+        for i, (src, dst) in enumerate(
+            [(q_hbm, q_v), (k_hbm, k_v), (v_hbm, v_v), (c_hbm, c_v), (w_hbm, w_v)]
+        )
+    ]
+    for load in loads:
+        load.start()
+
+    def remote(kind, d, src, dst):
+        return pltpu.make_async_remote_copy(
+            src_ref=src,
+            dst_ref=dst,
+            send_sem=send_sem.at[kind, d],
+            recv_sem=recv_sem.at[kind, d],
+            device_id={"ctx": peers[d]},
+            device_id_type=pl.DeviceIdType.MESH,
+        )
+
+    row_id = lax.broadcasted_iota(jnp.int32, (rows, rows), 0)
+    col_id = lax.broadcasted_iota(jnp.int32, (rows, rows), 1)
+    order = (col_id == R * (row_id % per) + row_id // per).astype(F32).astype(BF16)
+    left_row = lax.broadcasted_iota(jnp.int32, (1, LANES), 1) < DH
+
+    for load in loads[:3]:
+        load.wait()
+    for c in range(n):
+        cols = pl.ds(c * LANES, LANES)
+        picker = order[c * group : (c + 1) * group, :]
+        parts = []
+        for ref in (q_v, k_v, v_v):
+            picked = mm(picker, ref[:, cols], NN)
+            parts.append(jnp.where(left_row, picked[:per], picked[per:]))
+        parts.append(jnp.zeros_like(parts[0]))
+        qkv_send[c] = jnp.concatenate(parts, axis=0).astype(BF16)
+    loads[3].wait()
+    for c in range(n):
+        cols = pl.ds(c * LANES, LANES)
+        cot_send[c] = mm(order, c_v[:, cols], NN).astype(BF16)
+    qkv_recv[me] = qkv_send[me]
+    cot_recv[me] = cot_send[me]
+
+    pl.semaphore_wait(barrier, n - 1)
+    qkv_copies = [remote(0, d, qkv_send.at[peers[d]], qkv_recv.at[me]) for d in range(1, n)]
+    cot_copies = [remote(1, d, cot_send.at[peers[d]], cot_recv.at[me]) for d in range(1, n)]
+    for copy in qkv_copies:
+        copy.start()
+    for copy in cot_copies:
+        copy.start()
+    loads[4].wait()
+
+    for copy in qkv_copies:
+        copy.wait_recv()
+    got = qkv_recv[...].astype(F32)
+
+    def taken(j):
+        return got[:, j * per : (j + 1) * per, :].reshape(total, LANES)
+
+    def split(x):
+        zero = jnp.zeros_like(x)
+        return jnp.concatenate(
+            [jnp.where(left_row, x, zero), jnp.where(left_row, zero, x)], axis=0
+        )
+
+    def joined(x):
+        return jnp.where(left_row, x[:total], x[total:])
+
+    scale = DH ** (-0.5)
+    q_two = split(taken(0)).astype(BF16)
+    k_all = taken(1).astype(BF16)
+    v_all = taken(2).astype(BF16)
+    seg_rows = seg_devices * per
+    q_seg = (lax.broadcasted_iota(jnp.int32, (2 * total, total), 0) % total) // seg_rows
+    k_seg = lax.broadcasted_iota(jnp.int32, (2 * total, total), 1) // seg_rows
+    same = q_seg == k_seg
+    scores = jnp.where(same, mm(q_two, k_all, NT) * scale, -jnp.inf)
+    raised = jnp.exp(scores - jnp.max(scores, axis=-1, keepdims=True))
+    prob = raised / jnp.sum(raised, axis=-1, keepdims=True)
+    prob_16 = prob.astype(BF16)
+    attn = joined(mm(prob_16, v_all, NN)).astype(BF16)
+    attn_recv[me] = attn
+    attn_copies = [remote(2, d, attn_recv.at[me], attn_recv.at[me]) for d in range(1, n)]
+    for copy in attn_copies:
+        copy.start()
+
+    for copy in cot_copies:
+        copy.wait_recv()
+
+    def cot_group(c):
+        picked = cot_recv[:, pl.ds(pl.multiple_of(c * group, group), group), :]
+        return picked.reshape(n * group, LANES)
+
+    def tile(c):
+        return pl.ds(pl.multiple_of(c * LANES, LANES), LANES)
+
+    da_copies = []
+    own_da = None
+    for d in list(range(1, n)) + [0]:
+        c = peers[d]
+        both = mm(cot_group(c), w_v[:, tile(c)], NN).reshape(n, 2, per, LANES)
+        share = jnp.where(left_row, both[:, 0], both[:, 1]).reshape(total, LANES)
+        if d == 0:
+            own_da = share
+            continue
+        da_send[d] = share.astype(BF16)
+        copy = remote(3, d, da_send.at[d], da_recv.at[d])
+        copy.start()
+        da_copies.append(copy)
+
+    for d in range(n):
+        c = sources[d]
+        if d:
+            attn_copies[d - 1].wait_recv()
+        packed = attn_recv[c].astype(F32).reshape(n, per, LANES)
+        zero = jnp.zeros_like(packed)
+        wide = jnp.stack([jnp.where(left_row, packed, zero), jnp.where(left_row, zero, packed)], axis=1)
+        wide = wide.reshape(n * group, LANES).astype(BF16)
+        attn2[d] = wide
+        out = mm(wide, w_v[:, tile(c)], NT).astype(BF16)
+        pr_send[:, pl.ds(pl.multiple_of(c * group, group), group), :] = out.reshape(n, group, LANES)
+    pr_recv[me] = pr_send[me]
+    pr_copies = [remote(4, d, pr_send.at[peers[d]], pr_recv.at[me]) for d in range(1, n)]
+    for copy in pr_copies:
+        copy.start()
+
+    for copy in da_copies:
+        copy.wait_recv()
+    da = own_da
+    for d in range(1, n):
+        da = da + da_recv[d].astype(F32)
+    da_two = split(da).astype(BF16)
+    attn_two = split(attn.astype(F32))
+    delta = jnp.sum(da_two.astype(F32) * attn_two, axis=-1, keepdims=True)
+    d_score = (prob * (mm(da_two, v_all, NT) - delta)).astype(BF16)
+    dq = joined(mm(d_score, k_all, NN)) * scale
+    dk = mm(d_score, q_two, TN) * scale
+    dv = mm(prob_16, da_two, TN)
+    grads = [g.reshape(n, per, LANES) for g in (dq, dk, dv)]
+    grads.append(jnp.zeros_like(grads[0]))
+    dg_send[...] = jnp.concatenate(grads, axis=1).astype(BF16)
+    dg_recv[me] = dg_send[me]
+    dg_copies = [remote(5, d, dg_send.at[peers[d]], dg_recv.at[me]) for d in range(1, n)]
+    for copy in dg_copies:
+        copy.start()
+
+    for d in range(n):
+        c = sources[d]
+        wg_out[:, tile(c)] = mm(cot_group(c), attn2[d], TN)
+    stores = [
+        pltpu.make_async_copy(src, dst, out_sem.at[i])
+        for i, (src, dst) in enumerate(
+            [(wg_out, wg_hbm), (pr_out, proj_hbm), (dq_out, dq_hbm), (dk_out, dk_hbm), (dv_out, dv_hbm)]
+        )
+    ]
+    stores[0].start()
+
+    for copy in pr_copies:
+        copy.wait_recv()
+    for c in range(n):
+        pr_out[:, c * LANES : (c + 1) * LANES] = mm(order, pr_recv[c], TN).astype(BF16)
+    stores[1].start()
+
+    for copy in dg_copies:
+        copy.wait_recv()
+    head = lax.broadcasted_iota(jnp.int32, (R, LANES), 0)
+    lane_head = lax.broadcasted_iota(jnp.int32, (R, LANES), 1) // DH
+    for j, out in enumerate((dq_out, dk_out, dv_out)):
+        for c in range(n):
+            block = dg_recv[c].astype(F32)[j * per : (j + 1) * per]
+            here = (lane_head + 2 * c == head)[None]
+            spread_out = jnp.where(here, block[:, None, :], 0.0)
+            out[:, c * LANES : (c + 1) * LANES] = spread_out.reshape(rows, LANES).astype(BF16)
+        stores[2 + j].start()
+    for copy in qkv_copies + cot_copies + attn_copies + da_copies + pr_copies + dg_copies:
+        copy.wait_send()
+    for store in stores:
+        store.wait()
+
+
+def fused(queries, keys, values, cotangent, out_weight):
+    n = lax.axis_size("ctx")
+    rows = queries.shape[0]
+    per = rows // R
+    total = n * per
+    full = (rows, D)
+    square = (n, rows, LANES)
+    anywhere = pl.BlockSpec(memory_space=pl.ANY)
+    return pl.pallas_call(
+        functools.partial(fused_kernel, n, rows),
+        out_shape=(
+            jax.ShapeDtypeStruct(full, BF16),
+            jax.ShapeDtypeStruct((D // n, D), F32),
+            jax.ShapeDtypeStruct(full, BF16),
+            jax.ShapeDtypeStruct(full, BF16),
+            jax.ShapeDtypeStruct(full, BF16),
+        ),
+        in_specs=[anywhere] * 5,
+        out_specs=[anywhere] * 5,
+        scratch_shapes=[pltpu.VMEM(full, BF16)] * 4
+        + [pltpu.VMEM((D // n, D), BF16)]
+        + [
+            pltpu.VMEM((n, 4 * per, LANES), BF16),
+            pltpu.VMEM((n, 4 * per, LANES), BF16),
+            pltpu.VMEM(square, BF16),
+            pltpu.VMEM(square, BF16),
+            pltpu.VMEM((n, total, LANES), BF16),
+            pltpu.VMEM((n, total, LANES), BF16),
+            pltpu.VMEM((n, total, LANES), BF16),
+            pltpu.VMEM(square, BF16),
+            pltpu.VMEM(square, BF16),
+            pltpu.VMEM((n, 4 * per, LANES), BF16),
+            pltpu.VMEM((n, 4 * per, LANES), BF16),
+            pltpu.VMEM((n, n * 2 * per, LANES), BF16),
+            pltpu.VMEM(full, BF16),
+            pltpu.VMEM((D // n, D), F32),
+            pltpu.VMEM(full, BF16),
+            pltpu.VMEM(full, BF16),
+            pltpu.VMEM(full, BF16),
+            pltpu.SemaphoreType.DMA((6, n)),
+            pltpu.SemaphoreType.DMA((6, n)),
+            pltpu.SemaphoreType.DMA((5,)),
+            pltpu.SemaphoreType.DMA((5,)),
+        ],
+        compiler_params=pltpu.CompilerParams(
+            collective_id=0, has_side_effects=True, vmem_limit_bytes=40 * 1024 * 1024
+        ),
+    )(queries, keys, values, cotangent, out_weight)
+
+
 def solution(mesh):
     in_specs = (
         P(("dp", "ctx"), None),
@@ -161,4 +436,5 @@
         P(("dp", "ctx"), None),
         P(("dp", "ctx"), None),
     )
-    return jax.shard_map(shards, mesh=mesh, in_specs=in_specs, out_specs=out_specs, check_vma=False)
+    body = fused if fits(mesh) else shards
+    return jax.shard_map(body, mesh=mesh, in_specs=in_specs, out_specs=out_specs, check_vma=False)

time: 125 us -> 38.2 us (0.31)
  waiting for transfers between devices: 82.8 us -> 0 us
  Pallas kernels: 0 us -> 28.9 us
  between operations: 14.3 us -> 0.66 us
  matrix products: 7.71 us -> 0 us
  starting transfers between devices: 4.43 us -> 0 us
  local copies, waits for them, and re-layouts: 12.6 us -> 8.35 us
  other arithmetic: 2.47 us -> 0 us
    reduce_scatter x1 -> x0, waiting for transfers between devices: 42.6 us -> none  [shards(): lax.psum_scatter(lax.dot_general(cotangent, attention, (((0,), (0,)), (()...]
    all_gather x1 -> x0, waiting for transfers between devices: 29.4 us -> none  [shards(): full_weight = lax.all_gather(out_weight, 'ctx', axis=0, tiled=True)]
    pallas_call x0 -> x1, Pallas kernels: none -> 28.9 us  [fused(): pl.pallas_call(functools.partial(fused_kernel, n, rows), out_shape=(jax.S...]
    ppermute x6 -> x0, waiting for transfers between devices: 10.1 us -> none  [partner_2(): return lax.ppermute(value, axis, pairs)]
    dot_general x9 -> x0, matrix products: 7.71 us -> none  [the longest x1 2.66 us: shards(): lax.dot_general(cotangent, attention, (((0,), (0,)), ((), ())), preferred...]
    unnamed x5 -> x15, local copies, waits for them, and re-layouts: 2.05 us -> 8.35 us
    mul x4 -> x0, local copies, waits for them, and re-layouts: 5.82 us -> none  [dense_rows(): placed = sparse[:, None, :, :] * select_mask(sparse.dtype)]
    ppermute x6 -> x0, starting transfers between devices: 4.36 us -> none  [partner_2(): return lax.ppermute(value, axis, pairs)]
  transfers between devices with their start and end apart: 8 -> 0, of which waited for: 7 -> 0; matrix products, arithmetic and copies ran while one was open for 9% -> 0% of each run, Pallas kernels for 0% -> 0%
where the time goes in v1:
time: 38.2 us; the launch traced here: 37.9 us
  Pallas kernels  28.9 us (76%)
  local copies, waits for them, and re-layouts  8.35 us (22%)
  between operations  0.66 us (2%)
    pallas_call x1, Pallas kernels, fused(): pl.pallas_call(functools.partial(fused_kernel, n, rows), out_shape=(jax.S...  28.9 us
    unnamed x15, local copies, waits for them, and re-layouts  8.35 us

profile of v1, /device:TPU:0, one launch (start us, length us, event | category | flops | bytes accessed | tf_op | source)
XLA Modules:
  0.0 37.9 jit_solution(6541592563841233293)
XLA Ops:
  0.6 0.0 copy-start
  0.6 0.9 %copy-done = bf16[128,1024]{1,0:T(8,128)(2,1)S(1)} copy-done((bf16[128,1024]{1,0:T(8,128)(2,1)S(1)}, bf16[128,1024]{1,0:T(8,128)(2,1)}, u32[]{:S(2)}) %copy-start) | copy-done | bytes 262168
  1.6 0.0 copy-start.1
  1.6 0.9 %copy-done.1 = bf16[128,1024]{1,0:T(8,128)(2,1)S(1)} copy-done((bf16[128,1024]{1,0:T(8,128)(2,1)S(1)}, bf16[128,1024]{1,0:T(8,128)(2,1)}, u32[]{:S(2)}) %copy-start.1) | copy-done | bytes 262168
  2.5 0.0 copy-start.2
  2.5 0.9 %copy-done.2 = bf16[128,1024]{1,0:T(8,128)(2,1)S(1)} copy-done((bf16[128,1024]{1,0:T(8,128)(2,1)S(1)}, bf16[128,1024]{1,0:T(8,128)(2,1)}, u32[]{:S(2)}) %copy-start.2) | copy-done | bytes 262168
  3.5 0.0 copy-start.3
  3.5 0.9 %copy-done.3 = bf16[128,1024]{1,0:T(8,128)(2,1)S(1)} copy-done((bf16[128,1024]{1,0:T(8,128)(2,1)S(1)}, bf16[128,1024]{1,0:T(8,128)(2,1)}, u32[]{:S(2)}) %copy-start.3) | copy-done | bytes 262168
  4.4 0.0 copy-start.4
  4.4 0.9 %copy-done.4 = bf16[128,1024]{1,0:T(8,128)(2,1)S(1)} copy-done((bf16[128,1024]{1,0:T(8,128)(2,1)S(1)}, bf16[128,1024]{1,0:T(8,128)(2,1)}, u32[]{:S(2)}) %copy-start.4) | copy-done | bytes 262168
  5.4 28.9 %shard_map.92 = (bf16[128,1024]{1,0:T(8,128)(2,1)S(1)}, f32[128,1024]{1,0:T(8,128)S(1)}, bf16[128,1024]{1,0:T(8,128)(2,1)S(1)}, bf16[128,1024]{1,0:T(8,128)(2,1)S(1)}, bf16[128,1024]{1,0:T(8,128)(2,1)S(1)}) custom-call(bf16[128,1024]{1,0:T(8,128)(2,1)S(1)} %copy-done, bf16[128,1024]{1,0:T(8,128)(2,1)S(1)} %copy-done.1, bf16[128,1024]{1,0:T(8,128)(2,1)S(1)} %copy-done.2, ...), custom_call_target="tpu_custom_call" | custom-call | tf_op jit(solution)/shard_map/pallas_call | solution.py:382
  34.3 0.7 %copy.15 = bf16[128,1024]{1,0:T(8,128)(2,1)} copy(bf16[128,1024]{1,0:T(8,128)(2,1)S(1)} %get-tuple-element.10) | data formatting | bytes 524288
  35.0 0.8 %copy.16 = f32[128,1024]{1,0:T(8,128)} copy(f32[128,1024]{1,0:T(8,128)S(1)} %get-tuple-element.11) | data formatting | bytes 1048576
  35.8 0.7 %copy.17 = bf16[128,1024]{1,0:T(8,128)(2,1)} copy(bf16[128,1024]{1,0:T(8,128)(2,1)S(1)} %get-tuple-element.12) | data formatting | bytes 524288
  36.5 0.7 %copy.18 = bf16[128,1024]{1,0:T(8,128)(2,1)} copy(bf16[128,1024]{1,0:T(8,128)(2,1)S(1)} %get-tuple-element.13) | data formatting | bytes 524288
  37.2 0.7 %copy.19 = bf16[128,1024]{1,0:T(8,128)(2,1)} copy(bf16[128,1024]{1,0:T(8,128)(2,1)S(1)} %get-tuple-element.14) | data formatting | bytes 524288
Async XLA Ops:
  0.6 1.0 %copy-start = (bf16[128,1024]{1,0:T(8,128)(2,1)S(1)}, bf16[128,1024]{1,0:T(8,128)(2,1)}, u32[]{:S(2)}) copy-start(bf16[128,1024]{1,0:T(8,128)(2,1)} %q_hbm.1) | copy-start | bytes 786436
  1.6 0.9 %copy-start.1 = (bf16[128,1024]{1,0:T(8,128)(2,1)S(1)}, bf16[128,1024]{1,0:T(8,128)(2,1)}, u32[]{:S(2)}) copy-start(bf16[128,1024]{1,0:T(8,128)(2,1)} %k_hbm.1) | copy-start | bytes 786436
  2.5 0.9 %copy-start.2 = (bf16[128,1024]{1,0:T(8,128)(2,1)S(1)}, bf16[128,1024]{1,0:T(8,128)(2,1)}, u32[]{:S(2)}) copy-start(bf16[128,1024]{1,0:T(8,128)(2,1)} %v_hbm.1) | copy-start | bytes 786436
  3.5 0.9 %copy-start.3 = (bf16[128,1024]{1,0:T(8,128)(2,1)S(1)}, bf16[128,1024]{1,0:T(8,128)(2,1)}, u32[]{:S(2)}) copy-start(bf16[128,1024]{1,0:T(8,128)(2,1)} %c_hbm.1) | copy-start | bytes 786436
  4.4 0.9 %copy-start.4 = (bf16[128,1024]{1,0:T(8,128)(2,1)S(1)}, bf16[128,1024]{1,0:T(8,128)(2,1)}, u32[]{:S(2)}) copy-start(bf16[128,1024]{1,0:T(8,128)(2,1)} %w_hbm.1) | copy-start | bytes 786436

commit v2 on v1

--- a/solution.py
+++ b/solution.py
@@ -172,11 +172,10 @@
 def fused_kernel(
     n, rows,
     q_hbm, k_hbm, v_hbm, c_hbm, w_hbm,
-    proj_hbm, wg_hbm, dq_hbm, dk_hbm, dv_hbm,
+    pr_recv, dg_recv, wg_any,
     q_v, k_v, v_v, c_v, w_v,
     qkv_send, qkv_recv, cot_send, cot_recv, attn_recv, da_send, da_recv,
-    pr_send, pr_recv, dg_send, dg_recv, attn2,
-    pr_out, wg_out, dq_out, dk_out, dv_out,
+    pr_send, dg_send, attn2, wg_out,
     send_sem, recv_sem, in_sem, out_sem,
 ):
     per = rows // R
@@ -312,7 +311,8 @@
         attn2[d] = wide
         out = mm(wide, w_v[:, tile(c)], NT).astype(BF16)
         pr_send[:, pl.ds(pl.multiple_of(c * group, group), group), :] = out.reshape(n, group, LANES)
-    pr_recv[me] = pr_send[me]
+    keep_pr = pltpu.make_async_copy(pr_send.at[me], pr_recv.at[me], out_sem.at[0])
+    keep_pr.start()
     pr_copies = [remote(4, d, pr_send.at[peers[d]], pr_recv.at[me]) for d in range(1, n)]
     for copy in pr_copies:
         copy.start()
@@ -332,7 +332,8 @@
     grads = [g.reshape(n, per, LANES) for g in (dq, dk, dv)]
     grads.append(jnp.zeros_like(grads[0]))
     dg_send[...] = jnp.concatenate(grads, axis=1).astype(BF16)
-    dg_recv[me] = dg_send[me]
+    keep_dg = pltpu.make_async_copy(dg_send.at[me], dg_recv.at[me], out_sem.at[1])
+    keep_dg.start()
     dg_copies = [remote(5, d, dg_send.at[peers[d]], dg_recv.at[me]) for d in range(1, n)]
     for copy in dg_copies:
         copy.start()
@@ -340,33 +341,52 @@
     for d in range(n):
         c = sources[d]
         wg_out[:, tile(c)] = mm(cot_group(c), attn2[d], TN)
+    keep_wg = pltpu.make_async_copy(wg_out, wg_any, out_sem.at[2])
+    keep_wg.start()
+
+    for copy in pr_copies + dg_copies:
+        copy.wait_recv()
+    for copy in qkv_copies + cot_copies + attn_copies + da_copies + pr_copies + dg_copies:
+        copy.wait_send()
+    for keep in (keep_pr, keep_dg, keep_wg):
+        keep.wait()
+
+
+def finish_kernel(
+    n, rows,
+    pr_any, dg_any, wg_any,
+    proj_hbm, wg_hbm, dq_hbm, dk_hbm, dv_hbm,
+    pr_v, dg_v, pr_out, dq_out, dk_out, dv_out, in_sem, out_sem,
+):
+    per = rows // R
+    load_pr = pltpu.make_async_copy(pr_any, pr_v, in_sem.at[0])
+    load_dg = pltpu.make_async_copy(dg_any, dg_v, in_sem.at[1])
+    load_dg.start()
+    load_pr.start()
     stores = [
         pltpu.make_async_copy(src, dst, out_sem.at[i])
         for i, (src, dst) in enumerate(
-            [(wg_out, wg_hbm), (pr_out, proj_hbm), (dq_out, dq_hbm), (dk_out, dk_hbm), (dv_out, dv_hbm)]
+            [(wg_any, wg_hbm), (pr_out, proj_hbm), (dq_out, dq_hbm), (dk_out, dk_hbm), (dv_out, dv_hbm)]
         )
     ]
     stores[0].start()
-
-    for copy in pr_copies:
-        copy.wait_recv()
-    for c in range(n):
-        pr_out[:, c * LANES : (c + 1) * LANES] = mm(order, pr_recv[c], TN).astype(BF16)
-    stores[1].start()
-
-    for copy in dg_copies:
-        copy.wait_recv()
+    load_dg.wait()
     head = lax.broadcasted_iota(jnp.int32, (R, LANES), 0)
     lane_head = lax.broadcasted_iota(jnp.int32, (R, LANES), 1) // DH
     for j, out in enumerate((dq_out, dk_out, dv_out)):
         for c in range(n):
-            block = dg_recv[c].astype(F32)[j * per : (j + 1) * per]
+            block = dg_v[c].astype(F32)[j * per : (j + 1) * per]
             here = (lane_head + 2 * c == head)[None]
             spread_out = jnp.where(here, block[:, None, :], 0.0)
             out[:, c * LANES : (c + 1) * LANES] = spread_out.reshape(rows, LANES).astype(BF16)
         stores[2 + j].start()
-    for copy in qkv_copies + cot_copies + attn_copies + da_copies + pr_copies + dg_copies:
-        copy.wait_send()
+    row_id = lax.broadcasted_iota(jnp.int32, (rows, rows), 0)
+    col_id = lax.broadcasted_iota(jnp.int32, (rows, rows), 1)
+    order = (row_id == R * (col_id % per) + col_id // per).astype(F32).astype(BF16)
+    load_pr.wait()
+    for c in range(n):
+        pr_out[:, c * LANES : (c + 1) * LANES] = mm(order, pr_v[c], NN).astype(BF16)
+    stores[1].start()
     for store in stores:
         store.wait()
 
@@ -378,9 +398,45 @@
     total = n * per
     full = (rows, D)
     square = (n, rows, LANES)
+    compact = (n, 4 * per, LANES)
+    packed = (n, total, LANES)
     anywhere = pl.BlockSpec(memory_space=pl.ANY)
+    in_hbm = pl.BlockSpec(memory_space=pltpu.HBM)
+    room = 60 * 1024 * 1024
+    pieces = pl.pallas_call(
+        functools.partial(fused_kernel, n, rows),
+        out_shape=(
+            jax.ShapeDtypeStruct(square, BF16),
+            jax.ShapeDtypeStruct(compact, BF16),
+            jax.ShapeDtypeStruct((D // n, D), F32),
+        ),
+        in_specs=[in_hbm] * 5,
+        out_specs=[anywhere] * 3,
+        scratch_shapes=[pltpu.VMEM(full, BF16)] * 4
+        + [
+            pltpu.VMEM((D // n, D), BF16),
+            pltpu.VMEM(compact, BF16),
+            pltpu.VMEM(compact, BF16),
+            pltpu.VMEM(square, BF16),
+            pltpu.VMEM(square, BF16),
+            pltpu.VMEM(packed, BF16),
+            pltpu.VMEM(packed, BF16),
+            pltpu.VMEM(packed, BF16),
+            pltpu.VMEM(square, BF16),
+            pltpu.VMEM(compact, BF16),
+            pltpu.VMEM((n, n * 2 * per, LANES), BF16),
+            pltpu.VMEM((D // n, D), F32),
+            pltpu.SemaphoreType.DMA((6, n)),
+            pltpu.SemaphoreType.DMA((6, n)),
+            pltpu.SemaphoreType.DMA((5,)),
+            pltpu.SemaphoreType.DMA((3,)),
+        ],
+        compiler_params=pltpu.CompilerParams(
+            collective_id=0, has_side_effects=True, vmem_limit_bytes=room
+        ),
+    )(queries, keys, values, cotangent, out_weight)
     return pl.pallas_call(
-        functools.partial(fused_kernel, n, rows),
+        functools.partial(finish_kernel, n, rows),
         out_shape=(
             jax.ShapeDtypeStruct(full, BF16),
             jax.ShapeDtypeStruct((D // n, D), F32),
@@ -388,37 +444,13 @@
             jax.ShapeDtypeStruct(full, BF16),
             jax.ShapeDtypeStruct(full, BF16),
         ),
-        in_specs=[anywhere] * 5,
-        out_specs=[anywhere] * 5,
-        scratch_shapes=[pltpu.VMEM(full, BF16)] * 4
-        + [pltpu.VMEM((D // n, D), BF16)]
-        + [
-            pltpu.VMEM((n, 4 * per, LANES), BF16),
-            pltpu.VMEM((n, 4 * per, LANES), BF16),
-            pltpu.VMEM(square, BF16),
-            pltpu.VMEM(square, BF16),
-            pltpu.VMEM((n, total, LANES), BF16),
-            pltpu.VMEM((n, total, LANES), BF16),
-            pltpu.VMEM((n, total, LANES), BF16),
-            pltpu.VMEM(square, BF16),
-            pltpu.VMEM(square, BF16),
-            pltpu.VMEM((n, 4 * per, LANES), BF16),
-            pltpu.VMEM((n, 4 * per, LANES), BF16),
-            pltpu.VMEM((n, n * 2 * per, LANES), BF16),
-            pltpu.VMEM(full, BF16),
-            pltpu.VMEM((D // n, D), F32),
-            pltpu.VMEM(full, BF16),
-            pltpu.VMEM(full, BF16),
-            pltpu.VMEM(full, BF16),
-            pltpu.SemaphoreType.DMA((6, n)),
-            pltpu.SemaphoreType.DMA((6, n)),
-            pltpu.SemaphoreType.DMA((5,)),
-            pltpu.SemaphoreType.DMA((5,)),
-        ],
-        compiler_params=pltpu.CompilerParams(
-            collective_id=0, has_side_effects=True, vmem_limit_bytes=40 * 1024 * 1024
-        ),
-    )(queries, keys, values, cotangent, out_weight)
+        in_specs=[anywhere] * 3,
+        out_specs=[in_hbm] * 5,
+        scratch_shapes=[pltpu.VMEM(square, BF16), pltpu.VMEM(compact, BF16)]
+        + [pltpu.VMEM(full, BF16)] * 4
+        + [pltpu.SemaphoreType.DMA((2,)), pltpu.SemaphoreType.DMA((5,))],
+        compiler_params=pltpu.CompilerParams(vmem_limit_bytes=room),
+    )(*pieces)
 
 
 def solution(mesh):

time: 38.2 us -> 45.6 us (1.19)
  Pallas kernels: 28.9 us -> 44.8 us
  local copies, waits for them, and re-layouts: 8.35 us -> 0 us
    pallas_call x0 -> x1, Pallas kernels: none -> 17.1 us  [fused(): pl.pallas_call(functools.partial(finish_kernel, n, rows), out_shape=(jax....]
    unnamed x15 -> x0, local copies, waits for them, and re-layouts: 8.35 us -> none
    pallas_call x1, Pallas kernels: 28.9 us -> 27.8 us  [fused(): pl.pallas_call(functools.partial(fused_kernel, n, rows), out_shape=(jax.S...]
where the time goes in v2:
time: 45.6 us; the launch traced here: 45.5 us
  Pallas kernels  44.8 us (98%)
  between operations  0.64 us (1%)
    pallas_call x1, Pallas kernels, fused(): pl.pallas_call(functools.partial(fused_kernel, n, rows), out_shape=(jax.S...  27.8 us
    pallas_call x1, Pallas kernels, fused(): pl.pallas_call(functools.partial(finish_kernel, n, rows), out_shape=(jax....  17.1 us

profile of v2, /device:TPU:0, one launch (start us, length us, event | category | flops | bytes accessed | tf_op | source)
XLA Modules:
  0.0 45.5 jit_solution(12457168585503013504)
XLA Ops:
  0.6 27.8 %shard_map.92 = (bf16[8,128,128]{2,1,0:T(8,128)(2,1)}, bf16[8,32,128]{2,1,0:T(8,128)(2,1)}, f32[128,1024]{1,0:T(8,128)}) custom-call(bf16[128,1024]{1,0:T(8,128)(2,1)} %q_hbm.1, bf16[128,1024]{1,0:T(8,128)(2,1)} %k_hbm.1, bf16[128,1024]{1,0:T(8,128)(2,1)} %v_hbm.1, bf16[128,1024]{1,0:T(8,128)(2,1)} %c_hbm.1, bf16[128,1024]{1,0:T(8,128)(2,1)} %w_hbm.1), custom_call_target="tpu_custom_call" | custom-call | tf_op jit(solution)/shard_map/pallas_call | solution.py:406
  28.4 17.1 %shard_map.93 = (bf16[128,1024]{1,0:T(8,128)(2,1)}, f32[128,1024]{1,0:T(8,128)}, bf16[128,1024]{1,0:T(8,128)(2,1)}, bf16[128,1024]{1,0:T(8,128)(2,1)}, bf16[128,1024]{1,0:T(8,128)(2,1)}) custom-call(bf16[8,128,128]{2,1,0:T(8,128)(2,1)} %get-tuple-element.8.pr_any, bf16[8,32,128]{2,1,0:T(8,128)(2,1)} %get-tuple-element.9.dg_any, ...), custom_call_target="tpu_custom_call" | custom-call | tf_op jit(solution)/shard_map/pallas_call | solution.py:438

commit v3 on v2

--- a/solution.py
+++ b/solution.py
@@ -356,20 +356,21 @@
     n, rows,
     pr_any, dg_any, wg_any,
     proj_hbm, wg_hbm, dq_hbm, dk_hbm, dv_hbm,
-    pr_v, dg_v, pr_out, dq_out, dk_out, dv_out, in_sem, out_sem,
+    pr_v, dg_v, wg_v, pr_out, dq_out, dk_out, dv_out, in_sem, out_sem,
 ):
     per = rows // R
     load_pr = pltpu.make_async_copy(pr_any, pr_v, in_sem.at[0])
     load_dg = pltpu.make_async_copy(dg_any, dg_v, in_sem.at[1])
+    load_wg = pltpu.make_async_copy(wg_any, wg_v, in_sem.at[2])
     load_dg.start()
     load_pr.start()
+    load_wg.start()
     stores = [
         pltpu.make_async_copy(src, dst, out_sem.at[i])
         for i, (src, dst) in enumerate(
-            [(wg_any, wg_hbm), (pr_out, proj_hbm), (dq_out, dq_hbm), (dk_out, dk_hbm), (dv_out, dv_hbm)]
+            [(wg_v, wg_hbm), (pr_out, proj_hbm), (dq_out, dq_hbm), (dk_out, dk_hbm), (dv_out, dv_hbm)]
         )
     ]
-    stores[0].start()
     load_dg.wait()
     head = lax.broadcasted_iota(jnp.int32, (R, LANES), 0)
     lane_head = lax.broadcasted_iota(jnp.int32, (R, LANES), 1) // DH
@@ -383,6 +384,8 @@
     row_id = lax.broadcasted_iota(jnp.int32, (rows, rows), 0)
     col_id = lax.broadcasted_iota(jnp.int32, (rows, rows), 1)
     order = (row_id == R * (col_id % per) + col_id // per).astype(F32).astype(BF16)
+    load_wg.wait()
+    stores[0].start()
     load_pr.wait()
     for c in range(n):
         pr_out[:, c * LANES : (c + 1) * LANES] = mm(order, pr_v[c], NN).astype(BF16)
@@ -446,9 +449,9 @@
         ),
         in_specs=[anywhere] * 3,
         out_specs=[in_hbm] * 5,
-        scratch_shapes=[pltpu.VMEM(square, BF16), pltpu.VMEM(compact, BF16)]
+        scratch_shapes=[pltpu.VMEM(square, BF16), pltpu.VMEM(compact, BF16), pltpu.VMEM((D // n, D), F32)]
         + [pltpu.VMEM(full, BF16)] * 4
-        + [pltpu.SemaphoreType.DMA((2,)), pltpu.SemaphoreType.DMA((5,))],
+        + [pltpu.SemaphoreType.DMA((3,)), pltpu.SemaphoreType.DMA((5,))],
         compiler_params=pltpu.CompilerParams(vmem_limit_bytes=room),
     )(*pieces)
 

time: 45.6 us -> 30.7 us (0.67)
  Pallas kernels: 44.8 us -> 29.9 us
    pallas_call x1, Pallas kernels: 17.1 us -> 2.16 us  [fused(): pl.pallas_call(functools.partial(finish_kernel, n, rows), out_shape=(jax....]
where the time goes in v3:
time: 30.7 us; the launch traced here: 30.6 us
  Pallas kernels  29.9 us (97%)
  between operations  0.64 us (2%)
    pallas_call x1, Pallas kernels, fused(): pl.pallas_call(functools.partial(fused_kernel, n, rows), out_shape=(jax.S...  27.8 us
    pallas_call x1, Pallas kernels, fused(): pl.pallas_call(functools.partial(finish_kernel, n, rows), out_shape=(jax....  2.16 us

profile of v3, /device:TPU:0, one launch (start us, length us, event | category | flops | bytes accessed | tf_op | source)
XLA Modules:
  0.0 30.6 jit_solution(16952655204280944390)
XLA Ops:
  0.6 27.8 %shard_map.92 = (bf16[8,128,128]{2,1,0:T(8,128)(2,1)}, bf16[8,32,128]{2,1,0:T(8,128)(2,1)}, f32[128,1024]{1,0:T(8,128)}) custom-call(bf16[128,1024]{1,0:T(8,128)(2,1)} %q_hbm.1, bf16[128,1024]{1,0:T(8,128)(2,1)} %k_hbm.1, bf16[128,1024]{1,0:T(8,128)(2,1)} %v_hbm.1, bf16[128,1024]{1,0:T(8,128)(2,1)} %c_hbm.1, bf16[128,1024]{1,0:T(8,128)(2,1)} %w_hbm.1), custom_call_target="tpu_custom_call" | custom-call | tf_op jit(solution)/shard_map/pallas_call | solution.py:409
  28.4 2.2 %shard_map.93 = (bf16[128,1024]{1,0:T(8,128)(2,1)}, f32[128,1024]{1,0:T(8,128)}, bf16[128,1024]{1,0:T(8,128)(2,1)}, bf16[128,1024]{1,0:T(8,128)(2,1)}, bf16[128,1024]{1,0:T(8,128)(2,1)}) custom-call(bf16[8,128,128]{2,1,0:T(8,128)(2,1)} %get-tuple-element.8.pr_any, bf16[8,32,128]{2,1,0:T(8,128)(2,1)} %get-tuple-element.9.dg_any, ...), custom_call_target="tpu_custom_call" | custom-call | tf_op jit(solution)/shard_map/pallas_call | solution.py:441

commit v4 on v3

--- a/solution.py
+++ b/solution.py
@@ -174,7 +174,7 @@
     q_hbm, k_hbm, v_hbm, c_hbm, w_hbm,
     pr_recv, dg_recv, wg_any,
     q_v, k_v, v_v, c_v, w_v,
-    qkv_send, qkv_recv, cot_send, cot_recv, attn_recv, da_send, da_recv,
+    qkv_send, qkv_recv, cot_send, cot_recv, attn_recv, da_send, da_recv, da_mate, da_from_mate,
     pr_send, dg_send, attn2, wg_out,
     send_sem, recv_sem, in_sem, out_sem,
 ):
@@ -185,6 +185,8 @@
     me = lax.axis_index("ctx")
     peers = [lax.rem(me + d, n) for d in range(n)]
     sources = [lax.rem(me + n - d, n) for d in range(n)]
+    mate = me + 1 - 2 * lax.rem(me, 2)
+    far_first = sorted(range(1, n), key=lambda d: abs(d - n // 2))
 
     barrier = pltpu.get_barrier_semaphore()
     for d in range(1, n):
@@ -200,13 +202,13 @@
     for load in loads:
         load.start()
 
-    def remote(kind, d, src, dst):
+    def remote(kind, d, src, dst, to=None):
         return pltpu.make_async_remote_copy(
             src_ref=src,
             dst_ref=dst,
             send_sem=send_sem.at[kind, d],
             recv_sem=recv_sem.at[kind, d],
-            device_id={"ctx": peers[d]},
+            device_id={"ctx": peers[d] if to is None else to},
             device_id_type=pl.DeviceIdType.MESH,
         )
 
@@ -226,20 +228,23 @@
             parts.append(jnp.where(left_row, picked[:per], picked[per:]))
         parts.append(jnp.zeros_like(parts[0]))
         qkv_send[c] = jnp.concatenate(parts, axis=0).astype(BF16)
+    qkv_recv[me] = qkv_send[me]
+    pl.semaphore_wait(barrier, n - 1)
+    qkv_copies = [remote(0, d, qkv_send.at[peers[d]], qkv_recv.at[me]) for d in far_first]
+    for copy in qkv_copies:
+        copy.start()
+
+    def tile(c):
+        return pl.ds(pl.multiple_of(c * LANES, LANES), LANES)
+
     loads[3].wait()
-    for c in range(n):
-        cols = pl.ds(c * LANES, LANES)
-        cot_send[c] = mm(order, c_v[:, cols], NN).astype(BF16)
-    qkv_recv[me] = qkv_send[me]
-    cot_recv[me] = cot_send[me]
-
-    pl.semaphore_wait(barrier, n - 1)
-    qkv_copies = [remote(0, d, qkv_send.at[peers[d]], qkv_recv.at[me]) for d in range(1, n)]
-    cot_copies = [remote(1, d, cot_send.at[peers[d]], cot_recv.at[me]) for d in range(1, n)]
-    for copy in qkv_copies:
-        copy.start()
-    for copy in cot_copies:
-        copy.start()
+    cot_copies = []
+    for d in far_first:
+        cot_send[d] = mm(order, c_v[:, tile(peers[d])], NN).astype(BF16)
+        copy = remote(1, d, cot_send.at[d], cot_recv.at[me])
+        copy.start()
+        cot_copies.append(copy)
+    cot_recv[me] = mm(order, c_v[:, tile(me)], NN).astype(BF16)
     loads[4].wait()
 
     for copy in qkv_copies:
@@ -272,9 +277,18 @@
     prob_16 = prob.astype(BF16)
     attn = joined(mm(prob_16, v_all, NN)).astype(BF16)
     attn_recv[me] = attn
-    attn_copies = [remote(2, d, attn_recv.at[me], attn_recv.at[me]) for d in range(1, n)]
-    for copy in attn_copies:
-        copy.start()
+    across = [remote(2, d, attn_recv.at[me], attn_recv.at[me]) for d in range(2, n, 2)]
+    to_mate = remote(2, 1, attn_recv.at[me], attn_recv.at[me], mate)
+    for copy in across + [to_mate]:
+        copy.start()
+    passed = []
+    for i, d in enumerate(range(2, n, 2)):
+        across[i].wait_recv()
+        c = sources[d]
+        copy = remote(2, d + 1, attn_recv.at[c], attn_recv.at[c], mate)
+        copy.start()
+        passed.append(copy)
+    attn_copies = across + [to_mate] + passed
 
     for copy in cot_copies:
         copy.wait_recv()
@@ -283,27 +297,31 @@
         picked = cot_recv[:, pl.ds(pl.multiple_of(c * group, group), group), :]
         return picked.reshape(n * group, LANES)
 
-    def tile(c):
-        return pl.ds(pl.multiple_of(c * LANES, LANES), LANES)
-
+    def da_share(c):
+        both = mm(cot_group(c), w_v[:, tile(c)], NN).reshape(n, 2, per, LANES)
+        return jnp.where(left_row, both[:, 0], both[:, 1]).reshape(total, LANES)
+
+    chips = n // 2
+    for t in range(chips):
+        da_mate[t] = da_share(lax.rem(mate + 2 * t, n)).astype(BF16)
+    mate_copy = remote(3, 1, da_mate, da_from_mate, mate)
+    mate_copy.start()
+    shares = [da_share(peers[2 * t]) for t in range(chips)]
+    mate_copy.wait_recv()
     da_copies = []
-    own_da = None
-    for d in list(range(1, n)) + [0]:
-        c = peers[d]
-        both = mm(cot_group(c), w_v[:, tile(c)], NN).reshape(n, 2, per, LANES)
-        share = jnp.where(left_row, both[:, 0], both[:, 1]).reshape(total, LANES)
-        if d == 0:
-            own_da = share
-            continue
-        da_send[d] = share.astype(BF16)
-        copy = remote(3, d, da_send.at[d], da_recv.at[d])
+    for t in range(1, chips):
+        da_send[t] = (shares[t] + da_from_mate[t].astype(F32)).astype(BF16)
+        copy = remote(3, 2 * t, da_send.at[t], da_recv.at[t])
         copy.start()
         da_copies.append(copy)
-
-    for d in range(n):
-        c = sources[d]
-        if d:
-            attn_copies[d - 1].wait_recv()
+    own_da = shares[0] + da_from_mate[0].astype(F32)
+
+    pairs = [sources[d] for d in range(0, n, 2)] + [lax.rem(mate + n - d, n) for d in range(0, n, 2)]
+    for d, c in enumerate(pairs):
+        if d == chips:
+            to_mate.wait_recv()
+        elif d > chips:
+            passed[d - chips - 1].wait_recv()
         packed = attn_recv[c].astype(F32).reshape(n, per, LANES)
         zero = jnp.zeros_like(packed)
         wide = jnp.stack([jnp.where(left_row, packed, zero), jnp.where(left_row, zero, packed)], axis=1)
@@ -313,15 +331,15 @@
         pr_send[:, pl.ds(pl.multiple_of(c * group, group), group), :] = out.reshape(n, group, LANES)
     keep_pr = pltpu.make_async_copy(pr_send.at[me], pr_recv.at[me], out_sem.at[0])
     keep_pr.start()
-    pr_copies = [remote(4, d, pr_send.at[peers[d]], pr_recv.at[me]) for d in range(1, n)]
+    pr_copies = [remote(4, d, pr_send.at[peers[d]], pr_recv.at[me]) for d in far_first]
     for copy in pr_copies:
         copy.start()
 
     for copy in da_copies:
         copy.wait_recv()
     da = own_da
-    for d in range(1, n):
-        da = da + da_recv[d].astype(F32)
+    for t in range(1, chips):
+        da = da + da_recv[t].astype(F32)
     da_two = split(da).astype(BF16)
     attn_two = split(attn.astype(F32))
     delta = jnp.sum(da_two.astype(F32) * attn_two, axis=-1, keepdims=True)
@@ -338,15 +356,14 @@
     for copy in dg_copies:
         copy.start()
 
-    for d in range(n):
-        c = sources[d]
+    for d, c in enumerate(pairs):
         wg_out[:, tile(c)] = mm(cot_group(c), attn2[d], TN)
     keep_wg = pltpu.make_async_copy(wg_out, wg_any, out_sem.at[2])
     keep_wg.start()
 
     for copy in pr_copies + dg_copies:
         copy.wait_recv()
-    for copy in qkv_copies + cot_copies + attn_copies + da_copies + pr_copies + dg_copies:
+    for copy in qkv_copies + cot_copies + attn_copies + [mate_copy] + da_copies + pr_copies + dg_copies:
         copy.wait_send()
     for keep in (keep_pr, keep_dg, keep_wg):
         keep.wait()
@@ -403,6 +420,7 @@
     square = (n, rows, LANES)
     compact = (n, 4 * per, LANES)
     packed = (n, total, LANES)
+    half = (n // 2, total, LANES)
     anywhere = pl.BlockSpec(memory_space=pl.ANY)
     in_hbm = pl.BlockSpec(memory_space=pltpu.HBM)
     room = 60 * 1024 * 1024
@@ -423,8 +441,10 @@
             pltpu.VMEM(square, BF16),
             pltpu.VMEM(square, BF16),
             pltpu.VMEM(packed, BF16),
-            pltpu.VMEM(packed, BF16),
-            pltpu.VMEM(packed, BF16),
+            pltpu.VMEM(half, BF16),
+            pltpu.VMEM(half, BF16),
+            pltpu.VMEM(half, BF16),
+            pltpu.VMEM(half, BF16),
             pltpu.VMEM(square, BF16),
             pltpu.VMEM(compact, BF16),
             pltpu.VMEM((n, n * 2 * per, LANES), BF16),

time: 30.7 us -> 30.8 us (level)
  no operation moved by 1% of the time
where the time goes in v4:
time: 30.8 us; the launch traced here: 30.7 us
  Pallas kernels  30 us (97%)
  between operations  0.64 us (2%)
    pallas_call x1, Pallas kernels, fused(): pl.pallas_call(functools.partial(fused_kernel, n, rows), out_shape=(jax.S...  27.9 us
    pallas_call x1, Pallas kernels, fused(): pl.pallas_call(functools.partial(finish_kernel, n, rows), out_shape=(jax....  2.16 us

profile of v4, /device:TPU:0, one launch (start us, length us, event | category | flops | bytes accessed | tf_op | source)
XLA Modules:
  0.0 30.7 jit_solution(17837469846423015595)
XLA Ops:
  0.6 27.9 %shard_map.92 = (bf16[8,128,128]{2,1,0:T(8,128)(2,1)}, bf16[8,32,128]{2,1,0:T(8,128)(2,1)}, f32[128,1024]{1,0:T(8,128)}) custom-call(bf16[128,1024]{1,0:T(8,128)(2,1)} %q_hbm.1, bf16[128,1024]{1,0:T(8,128)(2,1)} %k_hbm.1, bf16[128,1024]{1,0:T(8,128)(2,1)} %v_hbm.1, bf16[128,1024]{1,0:T(8,128)(2,1)} %c_hbm.1, bf16[128,1024]{1,0:T(8,128)(2,1)} %w_hbm.1), custom_call_target="tpu_custom_call" | custom-call | tf_op jit(solution)/shard_map/pallas_call | solution.py:427
  28.5 2.2 %shard_map.93 = (bf16[128,1024]{1,0:T(8,128)(2,1)}, f32[128,1024]{1,0:T(8,128)}, bf16[128,1024]{1,0:T(8,128)(2,1)}, bf16[128,1024]{1,0:T(8,128)(2,1)}, bf16[128,1024]{1,0:T(8,128)(2,1)}) custom-call(bf16[8,128,128]{2,1,0:T(8,128)(2,1)} %get-tuple-element.8.pr_any, bf16[8,32,128]{2,1,0:T(8,128)(2,1)} %get-tuple-element.9.dg_any, ...), custom_call_target="tpu_custom_call" | custom-call | tf_op jit(solution)/shard_map/pallas_call | solution.py:461

commit v5 on v4

--- a/solution.py
+++ b/solution.py
@@ -281,15 +281,6 @@
     to_mate = remote(2, 1, attn_recv.at[me], attn_recv.at[me], mate)
     for copy in across + [to_mate]:
         copy.start()
-    passed = []
-    for i, d in enumerate(range(2, n, 2)):
-        across[i].wait_recv()
-        c = sources[d]
-        copy = remote(2, d + 1, attn_recv.at[c], attn_recv.at[c], mate)
-        copy.start()
-        passed.append(copy)
-    attn_copies = across + [to_mate] + passed
-
     for copy in cot_copies:
         copy.wait_recv()
 
@@ -307,6 +298,15 @@
     mate_copy = remote(3, 1, da_mate, da_from_mate, mate)
     mate_copy.start()
     shares = [da_share(peers[2 * t]) for t in range(chips)]
+    passed = []
+    for i, d in enumerate(range(2, n, 2)):
+        across[i].wait_recv()
+        c = sources[d]
+        copy = remote(2, d + 1, attn_recv.at[c], attn_recv.at[c], mate)
+        copy.start()
+        passed.append(copy)
+    attn_copies = across + [to_mate] + passed
+
     mate_copy.wait_recv()
     da_copies = []
     for t in range(1, chips):

time: 30.8 us -> 30 us (0.974)
  Pallas kernels: 30 us -> 29.2 us
    pallas_call x1, Pallas kernels: 27.9 us -> 27 us  [fused(): pl.pallas_call(functools.partial(fused_kernel, n, rows), out_shape=(jax.S...]
where the time goes in v5:
time: 30 us; the launch traced here: 29.8 us
  Pallas kernels  29.2 us (97%)
  between operations  0.64 us (2%)
    pallas_call x1, Pallas kernels, fused(): pl.pallas_call(functools.partial(fused_kernel, n, rows), out_shape=(jax.S...  27 us
    pallas_call x1, Pallas kernels, fused(): pl.pallas_call(functools.partial(finish_kernel, n, rows), out_shape=(jax....  2.16 us

profile of v5, /device:TPU:0, one launch (start us, length us, event | category | flops | bytes accessed | tf_op | source)
XLA Modules:
  0.0 29.8 jit_solution(14037450052363387305)
XLA Ops:
  0.6 27.0 %shard_map.92 = (bf16[8,128,128]{2,1,0:T(8,128)(2,1)}, bf16[8,32,128]{2,1,0:T(8,128)(2,1)}, f32[128,1024]{1,0:T(8,128)}) custom-call(bf16[128,1024]{1,0:T(8,128)(2,1)} %q_hbm.1, bf16[128,1024]{1,0:T(8,128)(2,1)} %k_hbm.1, bf16[128,1024]{1,0:T(8,128)(2,1)} %v_hbm.1, bf16[128,1024]{1,0:T(8,128)(2,1)} %c_hbm.1, bf16[128,1024]{1,0:T(8,128)(2,1)} %w_hbm.1), custom_call_target="tpu_custom_call" | custom-call | tf_op jit(solution)/shard_map/pallas_call | solution.py:427
  27.7 2.2 %shard_map.93 = (bf16[128,1024]{1,0:T(8,128)(2,1)}, f32[128,1024]{1,0:T(8,128)}, bf16[128,1024]{1,0:T(8,128)(2,1)}, bf16[128,1024]{1,0:T(8,128)(2,1)}, bf16[128,1024]{1,0:T(8,128)(2,1)}) custom-call(bf16[8,128,128]{2,1,0:T(8,128)(2,1)} %get-tuple-element.8.pr_any, bf16[8,32,128]{2,1,0:T(8,128)(2,1)} %get-tuple-element.9.dg_any, ...), custom_call_target="tpu_custom_call" | custom-call | tf_op jit(solution)/shard_map/pallas_call | solution.py:461

commit v6 on v5

--- a/solution.py
+++ b/solution.py
@@ -175,7 +175,7 @@
     pr_recv, dg_recv, wg_any,
     q_v, k_v, v_v, c_v, w_v,
     qkv_send, qkv_recv, cot_send, cot_recv, attn_recv, da_send, da_recv, da_mate, da_from_mate,
-    pr_send, dg_send, attn2, wg_out,
+    pr_send, pr_land, dg_send, attn2, wg_out,
     send_sem, recv_sem, in_sem, out_sem,
 ):
     per = rows // R
@@ -329,9 +329,8 @@
         attn2[d] = wide
         out = mm(wide, w_v[:, tile(c)], NT).astype(BF16)
         pr_send[:, pl.ds(pl.multiple_of(c * group, group), group), :] = out.reshape(n, group, LANES)
-    keep_pr = pltpu.make_async_copy(pr_send.at[me], pr_recv.at[me], out_sem.at[0])
-    keep_pr.start()
-    pr_copies = [remote(4, d, pr_send.at[peers[d]], pr_recv.at[me]) for d in far_first]
+    pr_land[me] = pr_send[me]
+    pr_copies = [remote(4, d, pr_send.at[peers[d]], pr_land.at[me]) for d in far_first]
     for copy in pr_copies:
         copy.start()
 
@@ -361,7 +360,11 @@
     keep_wg = pltpu.make_async_copy(wg_out, wg_any, out_sem.at[2])
     keep_wg.start()
 
-    for copy in pr_copies + dg_copies:
+    for copy in pr_copies:
+        copy.wait_recv()
+    keep_pr = pltpu.make_async_copy(pr_land, pr_recv, out_sem.at[0])
+    keep_pr.start()
+    for copy in dg_copies:
         copy.wait_recv()
     for copy in qkv_copies + cot_copies + attn_copies + [mate_copy] + da_copies + pr_copies + dg_copies:
         copy.wait_send()
@@ -446,6 +449,7 @@
             pltpu.VMEM(half, BF16),
             pltpu.VMEM(half, BF16),
             pltpu.VMEM(square, BF16),
+            pltpu.VMEM(square, BF16),
             pltpu.VMEM(compact, BF16),
             pltpu.VMEM((n, n * 2 * per, LANES), BF16),
             pltpu.VMEM((D // n, D), F32),

time: 30 us -> 30 us (level)
  no operation moved by 1% of the time
where the time goes in v6:
time: 30 us; the launch traced here: 29.8 us
  Pallas kernels  29.2 us (97%)
  between operations  0.64 us (2%)
    pallas_call x1, Pallas kernels, fused(): pl.pallas_call(functools.partial(fused_kernel, n, rows), out_shape=(jax.S...  27 us
    pallas_call x1, Pallas kernels, fused(): pl.pallas_call(functools.partial(finish_kernel, n, rows), out_shape=(jax....  2.16 us

profile of v6, /device:TPU:0, one launch (start us, length us, event | category | flops | bytes accessed | tf_op | source)
XLA Modules:
  0.0 29.8 jit_solution(5626931805536589612)
XLA Ops:
  0.6 27.0 %shard_map.92 = (bf16[8,128,128]{2,1,0:T(8,128)(2,1)}, bf16[8,32,128]{2,1,0:T(8,128)(2,1)}, f32[128,1024]{1,0:T(8,128)}) custom-call(bf16[128,1024]{1,0:T(8,128)(2,1)} %q_hbm.1, bf16[128,1024]{1,0:T(8,128)(2,1)} %k_hbm.1, bf16[128,1024]{1,0:T(8,128)(2,1)} %v_hbm.1, bf16[128,1024]{1,0:T(8,128)(2,1)} %c_hbm.1, bf16[128,1024]{1,0:T(8,128)(2,1)} %w_hbm.1), custom_call_target="tpu_custom_call" | custom-call | tf_op jit(solution)/shard_map/pallas_call | solution.py:430
  27.7 2.2 %shard_map.93 = (bf16[128,1024]{1,0:T(8,128)(2,1)}, f32[128,1024]{1,0:T(8,128)}, bf16[128,1024]{1,0:T(8,128)(2,1)}, bf16[128,1024]{1,0:T(8,128)(2,1)}, bf16[128,1024]{1,0:T(8,128)(2,1)}) custom-call(bf16[8,128,128]{2,1,0:T(8,128)(2,1)} %get-tuple-element.8.pr_any, bf16[8,32,128]{2,1,0:T(8,128)(2,1)} %get-tuple-element.9.dg_any, ...), custom_call_target="tpu_custom_call" | custom-call | tf_op jit(solution)/shard_map/pallas_call | solution.py:465
